TPU v7x, 128 devices: a whole 4x4x4 slice. The times are simulated.
128 devices in a mesh: inst: 16 (over y_lo, z, core), tp: 8 (over y_hi, x).
Axes of the slice: x: 4, y: 4 (y_hi: 2, y_lo: 2; y = y_hi * 2 + y_lo), z: 4, core: 2. Of those that a mesh axis runs over, the one named last changes fastest.
Arguments:
- hidden_rows: bfloat16 [8192, 8192], P('inst', 'tp'), may hold values from -48 to 48
- lengths: int32 [16, 4], P('inst'), may hold values from 1 to 256, 512 in all within a row
- attn_gain: float32 [8192], replicated, may hold values from 0.5 to 2
- w_joined: bfloat16 [16, 8192, 6144], P('inst', None, 'tp'), may hold values from -3 to 3, as said below
- w_out: bfloat16 [4096, 8192], P('tp'), may hold values from -0.75 to 0.75
Outputs:
- attention_out: bfloat16 [8192, 8192], P('inst', 'tp')
Inputs may be any that keep to these rules, and one draw needn't show every extreme that they name: `w_joined`: only index 0, the live instance, holds the layer that the steps use.
All inputs are finite; a program needn't handle non-finite values.
Results may differ from a plain program's by a relative error of at most 0.015.
Values may be sent and summed in bfloat16 or wider, within the bound.
A program may use at most 192 MiB of HBM per device.

v0:
```python
import math

import jax
import jax.numpy as jnp
from jax import lax
from jax.sharding import PartitionSpec as P

KVHEADS = 8
HD = 128
QHEADS = 32


EPSILON = 1e-05
ROPE_BASE = 500000.0
ROPE_FACTOR = 8.0
LOW_FACTOR = 1.0
HIGH_FACTOR = 4.0
OLD_CONTEXT = 8192.0


def spread(value, axis, source):
    kept = jnp.where(lax.axis_index(axis) == source, value, 0).astype(value.dtype)
    return lax.psum(kept, axis)


def rope_frequencies(head_size):
    indices = jnp.arange(head_size // 2, dtype=jnp.float32)
    base_freq = jnp.exp(indices * (-2.0 * math.log(ROPE_BASE) / head_size))
    wavelength = 2.0 * math.pi / base_freq
    blending = (OLD_CONTEXT / wavelength - LOW_FACTOR) / (HIGH_FACTOR - LOW_FACTOR)
    blended = (1.0 - blending) * base_freq / ROPE_FACTOR + blending * base_freq
    slowed = jnp.where(wavelength > OLD_CONTEXT / LOW_FACTOR, base_freq / ROPE_FACTOR, blended)
    return jnp.where(wavelength < OLD_CONTEXT / HIGH_FACTOR, base_freq, slowed)


def prompt_layout(counts, row_count):
    prompt_ends = jnp.cumsum(counts)
    prompt_starts = prompt_ends - counts
    row_index = jnp.arange(row_count, dtype=jnp.int32)
    segment = jnp.sum((row_index[:, None] >= prompt_ends[None, :]).astype(jnp.int32), axis=1)
    prompt_index = jnp.arange(counts.shape[0], dtype=jnp.int32)
    begins = jnp.sum(
        jnp.where(prompt_index[None, :] == segment[:, None], prompt_starts[None, :], 0), axis=1
    )
    return (segment, row_index - begins)


def rotate(values, cosine, sine_table):
    half_size = values.shape[-1] // 2
    first_half = values[..., :half_size]
    second_half = values[..., half_size:]
    return jnp.concatenate(
        [
            first_half * cosine - second_half * sine_table,
            second_half * cosine + first_half * sine_table,
        ],
        axis=-1,
    )


def local(hidden_rows, lengths, attn_gain, w_joined, w_out):
    row_count = hidden_rows.shape[0]
    heads_query = QHEADS // lax.axis_size("tp")
    heads_key = KVHEADS // lax.axis_size("tp")
    group_size = heads_query // heads_key
    query_cols = heads_query * HD
    key_cols = heads_key * HD
    gathered = lax.all_gather(hidden_rows, "tp", axis=1, tiled=True)
    gathered_wide = gathered.astype(jnp.float32)
    inverse = lax.rsqrt(jnp.mean(gathered_wide * gathered_wide, axis=1, keepdims=True) + EPSILON)
    scaled = (gathered_wide * attn_gain[None, :]).astype(jnp.bfloat16)
    joined_weight = spread(w_joined, "inst", 0)[0]
    projection = jnp.dot(scaled, joined_weight, preferred_element_type=jnp.float32)
    projection = projection * inverse
    segment, position = prompt_layout(lengths[0], row_count)
    angles = position.astype(jnp.float32)[:, None] * rope_frequencies(HD)[None, :]
    cosine = jnp.cos(angles)[:, None, :]
    sine_table = jnp.sin(angles)[:, None, :]
    query_heads = rotate(
        projection[:, :query_cols].reshape(row_count, heads_query, HD), cosine, sine_table
    ).astype(jnp.bfloat16)
    key_heads = rotate(
        projection[:, query_cols : query_cols + key_cols].reshape(row_count, heads_key, HD),
        cosine,
        sine_table,
    ).astype(jnp.bfloat16)
    value_heads = (
        projection[:, query_cols + key_cols :]
        .reshape(row_count, heads_key, HD)
        .astype(jnp.bfloat16)
    )
    grouped = query_heads.reshape(row_count, heads_key, group_size, HD)
    scores = jnp.einsum(
        "qkgd,skd->kgqs", grouped, key_heads, preferred_element_type=jnp.float32
    ) * (1.0 / math.sqrt(HD))
    row_index = jnp.arange(row_count, dtype=jnp.int32)
    allowed = (segment[:, None] == segment[None, :]) & (row_index[None, :] <= row_index[:, None])
    largest = jnp.max(jnp.where(allowed, scores, -1e30), axis=3, keepdims=True)
    weights = jnp.exp(jnp.where(allowed, scores - largest, -1e30))
    denominator = jnp.sum(weights, axis=3)
    mixed = jnp.einsum(
        "kgqs,skd->kgqd",
        weights.astype(jnp.bfloat16),
        value_heads,
        preferred_element_type=jnp.float32,
    )
    attended = mixed / denominator[..., None]
    attended = (
        jnp.transpose(attended, (2, 0, 1, 3)).reshape(row_count, query_cols).astype(jnp.bfloat16)
    )
    partial_out = jnp.dot(attended, w_out, preferred_element_type=jnp.float32).astype(jnp.bfloat16)
    return (
        lax.psum_scatter(partial_out, "tp", scatter_dimension=1, tiled=True)
        .astype(jnp.float32)
        .astype(jnp.bfloat16)
    )


def solution(mesh):
    return jax.shard_map(
        local,
        mesh=mesh,
        in_specs=(P("inst", "tp"), P("inst", None), P(), P("inst", None, "tp"), P("tp", None)),
        out_specs=P("inst", "tp"),
        check_vma=False,
    )
```

profile of v0, /device:TPU:1, one launch (start us, length us, event | category | flops | bytes accessed | tf_op | source)
XLA Modules:
  0.0 380.6 jit_solution(15813657198367728697)
XLA Ops:
  7.4 0.0 all-gather.2.cloned.1.call-start
  7.4 0.7 all-gather.2.cloned.1.call-update
  8.1 0.0 all-reduce.2.cloned.1.call-start
  8.1 5.6 %select_bitcast_fusion = bf16[8192,768]{1,0:T(8,128)(2,1)} fusion(bf16[1,8192,768]{2,1,0:T(8,128)(2,1)} %param.8, pred[]{:T(512)S(6)} %eq.32), kind=kLoop, calls=%fused_computation.4 | loop fusion | flops 6291456 | bytes 25165824 | tf_op jit(solution)/shard_map/squeeze | solution.py:72
  13.7 0.0 all-reduce.2.cloned.1.call-update
  13.7 0.0 reduce-scatter.2.cloned.1.call-start
  13.8 0.6 copy-done.2
  14.4 0.2 reduce-window.4
  14.6 0.1 convert_reduce_fusion
  14.7 0.1 select_reduce_fusion
  14.8 0.2 fusion.17
  15.0 1.0 multiply_cosine_fusion
  16.0 0.0 copy-start.1
  16.0 106.0 %all-gather.2.cloned.1.call-done = bf16[512,8192]{1,0:T(8,128)(2,1)} async-done(((bf16[512,1024]{1,0:T(8,128)(2,1)}), bf16[512,8192]{1,0:T(8,128)(2,1)}) %all-gather.2.cloned.1.call-update) | async-done | bytes 8388624 | tf_op jit(solution)/shard_map/all_gather | solution.py:68
  121.9 5.3 %fusion.1 = f32[512]{0:T(512)S(1)} fusion(bf16[512,8192]{1,0:T(8,128)(2,1)} %all-gather.2.cloned.1.call-done), kind=kLoop, calls=%fused_computation.3 | loop fusion | flops 12582400 | bytes 8390656 | tf_op jit(solution)/shard_map/reduce_sum | solution.py:70
  127.2 103.5 %all-reduce.2.cloned.1.call-done = bf16[8192,768]{1,0:T(8,128)(2,1)} async-done(((bf16[8192,768]{1,0:T(8,128)(2,1)}), bf16[8192,768]{1,0:T(8,128)(2,1)}) %all-reduce.2.cloned.1.call-update) | async-done | bytes 12582928 | tf_op jit(solution)/shard_map/psum | solution.py:23
  230.7 0.0 copy-done.1
  230.7 12.1 %fusion.14 = f32[512,768]{1,0:T(8,128)S(1)} fusion(bf16[8192,768]{1,0:T(8,128)(2,1)} %all-reduce.2.cloned.1.call-done, bf16[512,8192]{1,0:T(8,128)(2,1)} %all-gather.2.cloned.1.call-done, f32[8192]{0:T(1024)S(1)} %copy-done.1, f32[512]{0:T(512)S(1)} %add_rsqrt_fusion), kind=kOutput, calls=%fused_computation.18 | convolution fusion | flops 6455427072 | bytes 22579200 | tf_op jit(solution)/shard_map/dot_general | solution.py:73
  242.8 0.1 slice.32
  242.9 1.0 copy-done
  243.9 0.4 reshape.197
  244.3 0.6 fusion.42
  244.9 1.2 fusion.37
  246.1 0.3 subtract_convert_fusion
  246.4 0.0 slice-start
  246.4 1.2 fusion.5
  247.6 0.9 fusion.8
  248.6 0.0 slice-start.1
  248.6 2.3 divide_convert_fusion
  250.9 7.0 %convolution_convert_fusion = bf16[512,8192]{1,0:T(8,128)(2,1)} fusion(bf16[512,512]{0,1:T(8,128)(2,1)S(1)} %bitcast.59, bf16[512,8192]{1,0:T(8,128)(2,1)S(1)} %bitcast.58), kind=kOutput, calls=%fused_computation.5 | convolution fusion | flops 4299161600 | bytes 17301504 | tf_op jit(solution)/shard_map/dot_general | solution.py:111
  257.9 0.0 reduce-scatter.2.cloned.1.call-update
  257.9 115.3 %reduce-scatter.2.cloned.1.call-done = bf16[512,1024]{1,0:T(8,128)(2,1)} async-done(((bf16[512,8192]{1,0:T(8,128)(2,1)}), bf16[512,1024]{1,0:T(8,128)(2,1)}) %reduce-scatter.2.cloned.1.call-update) | async-done | bytes 1048592 | tf_op jit(solution)/shard_map/reduce_scatter | solution.py:113
  (10 shorter events, 0.1 us)
Async XLA Ops:
  7.4 114.6 %all-gather.2.cloned.1.call-start = ((), (), s32[]{:S(2)}) async-start(), calls=%async_computation.1 | async-start | bytes 9437184 | tf_op jit(solution)/shard_map/all_gather | solution.py:68
  8.1 222.6 %all-reduce.2.cloned.1.call-start = ((), (), s32[]{:S(2)}) async-start(), calls=%async_computation.2 | async-start | bytes 25165824 | tf_op jit(solution)/shard_map/psum | solution.py:23
  13.7 0.7 copy-start.2
  13.7 359.4 %reduce-scatter.2.cloned.1.call-start = ((), (), s32[]{:S(2)}) async-start(), calls=%async_computation.3 | async-start | bytes 9437184 | tf_op jit(solution)/shard_map/reduce_scatter | solution.py:113
  16.0 214.7 %copy-start.1 = (f32[8192]{0:T(1024)S(1)}, f32[8192]{0:T(1024)}, u32[]{:S(2)}) copy-start(f32[8192]{0:T(1024)} %param.7) | copy-start | bytes 98308
  242.8 1.2 copy-start
  246.4 4.4 %slice-start = ((s8[8388608]{0:T(1024)(128)(4,1)}), s8[4194304]{0:T(1024)(128)(4,1)S(1)}, s32[]{:S(2)}) async-start(s8[8388608]{0:T(1024)(128)(4,1)} %bitcast.57), calls=%async_computation.4 | async-start | bytes 8388608
  248.6 2.3 slice-start.1
Sparse Core Ops, SparseCore 0:
  10.5 111.3 all-gather.1
  258.0 115.0 reduce-scatter.1
Sparse Core Ops, SparseCore 1:
  13.8 216.8 all-reduce.1
where the time goes:
time: 381 us
  waiting for transfers between devices  325 us (85%)
  matrix products  22.5 us (6%)
  between operations  15 us (4%)
  other arithmetic  14.8 us (4%)
    reduce_scatter x1, waiting for transfers between devices, local(): lax.psum_scatter(partial_out, 'tp', scatter_dimension=1, tiled=True)  115 us
    all_gather x1, waiting for transfers between devices, local(): gathered = lax.all_gather(hidden_rows, 'tp', axis=1, tiled=True)  106 us
    psum x1, waiting for transfers between devices, spread(): return lax.psum(kept, axis)  103 us
    dot_general x1, matrix products, local(): jnp.dot(scaled, joined_weight, preferred_element_type=jnp.float32)  12.1 us
  transfers between devices with their start and end apart: 3, of which 3 were waited for; matrix products, arithmetic and copies ran while one was open for 3% of the time, Pallas kernels for 0%

commit v1 on v0

v1 whole, which is shorter than its diff:
```python
import functools
import math

import jax
import jax.numpy as jnp
from jax import lax
from jax.experimental import pallas as pl
from jax.experimental.pallas import tpu as pltpu
from jax.sharding import PartitionSpec as P

MESH = pl.DeviceIdType.MESH
F32 = jnp.float32
BF16 = jnp.bfloat16

KVHEADS = 8
HD = 128
QHEADS = 32
ROWS = 512
D = 8192
N_TP = 8
FEATS = D // N_TP
COLS = 768
HEADS = QHEADS // N_TP
ATT_COLS = HEADS * HD
LONGEST = 256

EPSILON = 1e-05
ROPE_BASE = 500000.0
ROPE_FACTOR = 8.0
LOW_FACTOR = 1.0
HIGH_FACTOR = 4.0
OLD_CONTEXT = 8192.0

CHUNK = 32
TREE_STEPS = (43, 43, 42)
TREE_BASE = (0, 2752, 5504)
GRAY = (0, 1, 3, 2)
LAG = 4
N_SLOTS = max(TREE_STEPS) + 4 * LAG

PIECE = 128
N_PIECES = ROWS // PIECE
TQ = 128
N_Q = ROWS // TQ


def tree_masks():
    masks = [[0] * 3 for _ in range(3)]
    depths = [0] * 3
    node_of = {}
    for y_lo in range(2):
        for z in range(4):
            node_of[y_lo * 4 + GRAY[z]] = y_lo * 4 + z
    first_edges = [(0, 0), (1, 1), (1, 2), (3, 2), (3, 0), (5, 0), (7, 0)]
    for tree in range(3):
        depth = {0: 0}
        for code, dim in first_edges:
            depth[code ^ (1 << dim)] = depth[code] + 1
            turned = ((code << tree) | (code >> (3 - tree))) & 7
            masks[tree][(dim + tree) % 3] |= 1 << node_of[turned]
        for code, far in depth.items():
            turned = ((code << tree) | (code >> (3 - tree))) & 7
            depths[tree] |= far << (3 * node_of[turned])
    return masks, depths


MASKS, DEPTHS = tree_masks()


def rope_tables(start_of, rows):
    lane = lax.broadcasted_iota(jnp.int32, (1, HD), 1)
    index = lax.rem(lane, HD // 2).astype(F32)
    base = jnp.exp(index * (-2.0 * math.log(ROPE_BASE) / HD))
    wavelength = 2.0 * math.pi / base
    blending = (OLD_CONTEXT / wavelength - LOW_FACTOR) / (HIGH_FACTOR - LOW_FACTOR)
    blended = (1.0 - blending) * base / ROPE_FACTOR + blending * base
    slowed = jnp.where(wavelength > OLD_CONTEXT / LOW_FACTOR, base / ROPE_FACTOR, blended)
    frequency = jnp.where(wavelength < OLD_CONTEXT / HIGH_FACTOR, base, slowed)
    row = lax.broadcasted_iota(jnp.int32, (rows, HD), 0)
    angles = (row - start_of(row)).astype(F32) * frequency
    sine = jnp.sin(angles)
    return jnp.cos(angles), jnp.where(lane < HD // 2, -sine, sine)


def body(
    hidden, lengths, gain, w_in, wo_in, out,
    w, xs, wo, acc, att, pf, rb, own, sums, inv, cosine, sine, qb, kb, vb,
    recv_w, send_w, send_sib, recv_x, send_x, recv_s, send_s,
    recv_wx, send_wx, recv_wz, send_wz, recv_ws, send_ws, loc_wo,
    recv_a, send_a, recv_y, send_y,
):
    inst = lax.axis_index("inst")
    tp = lax.axis_index("tp")
    core = lax.rem(inst, 2)
    z = lax.rem(inst // 2, 4)
    y_lo = inst // 8
    x = lax.rem(tp, 4)
    y_hi = tp // 4

    def inst_of(y_lo_, z_, core_):
        return (y_lo_ * 4 + z_) * 2 + core_

    right = (inst, y_hi * 4 + lax.rem(x + 1, 4))
    left = (inst, y_hi * 4 + lax.rem(x + 3, 4))
    across = (inst, y_hi * 4 + lax.rem(x + 2, 4))
    opposite = (inst, (1 - y_hi) * 4 + x)
    sibling = (inst_of(y_lo, z, 1 - core), tp)
    dims = (
        (inst_of(y_lo, z + 1 - 2 * lax.rem(z, 2), core), tp),
        (inst_of(y_lo, 3 - z, core), tp),
        (inst_of(1 - y_lo, z, core), tp),
    )
    z_others = [(inst_of(y_lo, lax.rem(z + k, 4), core), tp) for k in (1, 2, 3)]
    node = y_lo * 4 + z
    source_chip = node == 0
    is_source = jnp.logical_and(source_chip, core == 0)

    def send(src, dst, s_sem, r_sem, to):
        return pltpu.make_async_remote_copy(
            src_ref=src, dst_ref=dst, send_sem=s_sem, recv_sem=r_sem, device_id=to, device_id_type=MESH
        )

    def chunk(tree, step, parity):
        at = TREE_BASE[tree] + (2 * step + parity) * CHUNK
        return pl.ds(pl.multiple_of(at, CHUNK), CHUNK)

    barrier = pltpu.get_barrier_semaphore()
    peers = [(inst, lax.rem(tp + k, N_TP)) for k in range(1, N_TP)]
    greeted = peers + z_others + [sibling, dims[2]]
    for other in greeted:
        pl.semaphore_signal(barrier, inc=1, device_id=other, device_id_type=MESH)

    @pl.when(is_source)
    def _():
        for tree in range(3):

            def load(step, carry, tree=tree):
                for parity in range(2):
                    rows = chunk(tree, step, parity)
                    pltpu.make_async_copy(
                        w_in.at[0, rows], w.at[rows], recv_w.at[tree, step, parity]
                    ).start()
                return carry

            lax.fori_loop(0, TREE_STEPS[tree], load, 0)

    foreign_cols = pl.ds(pl.multiple_of(((1 - y_hi) * 4 + x) * FEATS, FEATS), FEATS)
    own_cols = pl.ds(pl.multiple_of(tp * FEATS, FEATS), FEATS)
    wo_local = (
        pltpu.make_async_copy(wo_in.at[:, foreign_cols], wo.at[0, :, pl.ds(0, FEATS)], loc_wo.at[0]),
        pltpu.make_async_copy(wo_in.at[:, own_cols], wo.at[0, :, pl.ds(FEATS, FEATS)], loc_wo.at[1]),
    )
    for copy in wo_local:
        copy.start()

    eye = (
        lax.broadcasted_iota(jnp.int32, (128, 128), 0) == lax.broadcasted_iota(jnp.int32, (128, 128), 1)
    ).astype(F32)
    sums[tp] = jnp.zeros((8, 128), F32)
    for g in range(4):
        wide = hidden[pl.ds(g * 128, 128), :].astype(F32)
        xs[0, pl.ds(g * 128, 128), :] = (wide * gain[...]).astype(BF16)
        column = jnp.sum(wide * wide, axis=1, keepdims=True)
        sums[tp, pl.ds(g, 1), :] = jnp.sum(column * eye, axis=0, keepdims=True)

    pl.semaphore_wait(barrier, len(greeted))

    def piece(slot, p):
        return xs.at[slot, pl.ds(p * PIECE, PIECE)]

    def send_piece(src_slot, dst_slot, p, sem, to):
        send(piece(src_slot, p), piece(dst_slot, p), send_x.at[sem], recv_x.at[dst_slot, p], to).start()

    def wait_piece(slot, p):
        pltpu.make_async_copy(piece(slot, p), piece(slot, p), recv_x.at[slot, p]).wait()

    for p in range(N_PIECES):
        send_piece(0, 4, p, 2, opposite)
        send_piece(0, 2, p, 0, right)
        send_piece(0, 1, p, 1, left)
    for other in peers:
        send(sums.at[tp], sums.at[tp], send_s, recv_s.at[tp], other).start()

    wo_rows = pl.ds(pl.multiple_of(z * 128 + core * 64, 64), 64)
    wo_targets = ((2, right, 1), (1, left, 3), (3, across, 2))
    for slot, to, shift in wo_targets:
        x_to = lax.rem(x + shift, 4)
        for part, y_part in ((0, 1 - y_hi), (1, y_hi)):
            cols = pl.ds(pl.multiple_of((y_part * 4 + x_to) * FEATS, FEATS), FEATS)
            send(
                wo_in.at[wo_rows, cols],
                wo.at[slot, wo_rows, pl.ds(part * FEATS, FEATS)],
                send_wx.at[slot - 1, part],
                recv_wx.at[slot - 1, part],
                to,
            ).start()

    sends_tree = [
        [((MASKS[tree][dim] >> node) & 1) == 1 for dim in range(3)] for tree in range(3)
    ]

    def weight_tree(tree, step):
        mine = chunk(tree, step, core)
        pltpu.make_async_copy(w.at[mine], w.at[mine], recv_w.at[tree, step, core]).wait()
        for dim in range(3):
            if MASKS[tree][dim]:

                @pl.when(sends_tree[tree][dim])
                def _(dim=dim):
                    send(w.at[mine], w.at[mine], send_w.at[dim], recv_w.at[tree, step, core], dims[dim]).start()

        @pl.when(jnp.logical_or(jnp.logical_not(source_chip), core == 0))
        def _():
            send(w.at[mine], w.at[mine], send_sib, recv_w.at[tree, step, core], sibling).start()

        @pl.when(is_source)
        def _():
            theirs = chunk(tree, step, 1)
            pltpu.make_async_copy(w.at[theirs], w.at[theirs], recv_w.at[tree, step, 1]).wait()
            send(w.at[theirs], w.at[theirs], send_sib, recv_w.at[tree, step, 1], sibling).start()

    def weight_steps(low, high):
        def slot_of(slot, carry):
            for tree in range(3):
                step = slot - LAG * ((DEPTHS[tree] >> (3 * node)) & 7)

                @pl.when(jnp.logical_and(step >= 0, step < TREE_STEPS[tree]))
                def _(tree=tree, step=step):
                    weight_tree(tree, step)

            return carry

        lax.fori_loop(low, high, slot_of, 0)

    def relay_ring(h, e):
        wait_piece(4 * h + 2, e)
        send_piece(4 * h + 2, 4 * h + 3, e, 0, right)
        wait_piece(4 * h + 1, 2 + e)
        send_piece(4 * h + 1, 4 * h + 3, 2 + e, 1, left)

    def relay_opposite(p):
        wait_piece(4, p)
        send_piece(4, 6, p, 0, right)
        send_piece(4, 5, p, 1, left)

    def wo_spread():
        for slot in range(3):
            for part in range(2):
                dst = wo.at[slot + 1, wo_rows, pl.ds(part * FEATS, FEATS)]
                pltpu.make_async_copy(dst, dst, recv_wx.at[slot, part]).wait()
        block = wo.at[pl.ds(1, 3), wo_rows, :]
        for k, to in enumerate(z_others):
            send(block, block, send_wz.at[k], recv_wz.at[k], to).start()
        send(block, block, send_ws.at[3], recv_ws.at[3], sibling).start()

    weight_steps(0, 22)
    relay_ring(0, 0)
    relay_ring(0, 1)
    weight_steps(22, 28)
    relay_opposite(0)
    weight_steps(28, 32)
    relay_opposite(1)
    weight_steps(32, 36)
    relay_opposite(2)
    weight_steps(36, 40)
    relay_opposite(3)
    weight_steps(40, 48)
    relay_ring(1, 0)
    weight_steps(48, 52)
    relay_ring(1, 1)
    weight_steps(52, N_SLOTS)
    wo_spread()

    length = [lengths[0, k] for k in range(3)]
    begins = [length[0], length[0] + length[1], length[0] + length[1] + length[2]]

    def start_of(row):
        start = jnp.zeros_like(row)
        for begin in begins:
            start = jnp.where(row >= begin, begin, start)
        return start

    cosine[...], sine[...] = rope_tables(start_of, ROWS)

    for tree in range(3):

        def others(step, carry, tree=tree):
            @pl.when(jnp.logical_not(is_source))
            def _():
                theirs = chunk(tree, step, 1 - core)
                pltpu.make_async_copy(w.at[theirs], w.at[theirs], recv_w.at[tree, step, 1 - core]).wait()

            return carry

        lax.fori_loop(0, TREE_STEPS[tree], others, 0)

    acc[...] = jnp.zeros_like(acc)

    def block_dot(slot, carry):
        turn = lax.rem(slot, 4)
        h = slot // 4

        for p in range(N_PIECES):
            seen = (turn == 0) | ((turn == 2) & (p < 2)) | ((turn == 1) & (p >= 2))

            @pl.when(jnp.logical_not(seen))
            def _(p=p):
                wait_piece(slot, p)

        shift = jnp.where(turn == 2, 3, jnp.where(turn == 3, 2, turn))
        owner = lax.rem(y_hi + h, 2) * 4 + lax.rem(x + shift, 4)
        base = pl.multiple_of(owner * FEATS, FEATS)
        for n in range(3):
            cols = pl.ds(n * 256, 256)
            acc[:, cols] += jnp.dot(
                xs[slot], w[pl.ds(base, FEATS), cols], preferred_element_type=F32
            )
        return carry

    lax.fori_loop(0, 8, block_dot, 0)

    for k in range(1, N_TP):
        sender = lax.rem(tp + k, N_TP)
        pltpu.make_async_copy(sums.at[sender], sums.at[sender], recv_s.at[sender]).wait()
    total = sums[0]
    for t in range(1, N_TP):
        total = total + sums[t]
    factor = lax.rsqrt(total * (1.0 / D) + EPSILON)
    for g in range(4):
        inv[pl.ds(g * 128, 128), :] = jnp.sum(factor[g : g + 1, :] * eye, axis=1, keepdims=True) * jnp.ones(
            (1, 128), F32
        )

    def turned(value, rows):
        return value * cosine[rows, :] + pltpu.roll(value, HD // 2, axis=1) * sine[rows, :]

    def split(g, carry):
        rows = pl.ds(pl.multiple_of(g * 128, 128), 128)
        scale = inv[rows, :]
        for head in range(HEADS):
            qb[head, rows, :] = turned(acc[rows, pl.ds(head * HD, HD)] * scale, rows).astype(BF16)
        kb[rows, :] = turned(acc[rows, pl.ds(ATT_COLS, HD)] * scale, rows).astype(BF16)
        vb[rows, :] = (acc[rows, pl.ds(ATT_COLS + HD, HD)] * scale).astype(BF16)
        return carry

    lax.fori_loop(0, 4, split, 0)

    def att_rows(slot, q):
        return att.at[slot, pl.ds(q * TQ, TQ)]

    def att_half(slot, q, half):
        return att.at[slot, pl.ds(q * TQ + half * (TQ // 2), TQ // 2)]

    for q in range(N_Q):
        low = max(0, q * TQ - LONGEST)
        high = (q + 1) * TQ
        row = lax.broadcasted_iota(jnp.int32, (TQ, high - low), 0) + q * TQ
        key = lax.broadcasted_iota(jnp.int32, (TQ, high - low), 1) + low
        allowed = (key <= row) & (key >= start_of(row))
        for head in range(HEADS):
            scores = lax.dot_general(
                qb[head, pl.ds(q * TQ, TQ), :],
                kb[pl.ds(low, high - low), :],
                (((1,), (1,)), ((), ())),
                preferred_element_type=F32,
            ) * (1.0 / math.sqrt(HD))
            scores = jnp.where(allowed, scores, -1e30)
            largest = jnp.max(scores, axis=1, keepdims=True)
            weights = jnp.exp(jnp.where(allowed, scores - largest, -1e30))
            denominator = jnp.sum(weights, axis=1, keepdims=True)
            mixed = jnp.dot(weights.astype(BF16), vb[pl.ds(low, high - low), :], preferred_element_type=F32)
            att[0, pl.ds(q * TQ, TQ), pl.ds(head * HD, HD)] = (mixed / denominator).astype(BF16)
        send(att_rows(0, q), att_rows(2, q), send_a.at[0], recv_a.at[1, q], right).start()
        send(att_rows(0, q), att_rows(1, q), send_a.at[1], recv_a.at[0, q], left).start()

    for copy in wo_local:
        copy.wait()
    for k in range(3):
        z_from = lax.rem(z + 3 - k, 4)
        rows = pl.ds(pl.multiple_of(z_from * 128 + core * 64, 64), 64)
        block = wo.at[pl.ds(1, 3), rows, :]
        pltpu.make_async_copy(block, block, recv_wz.at[k]).wait()
        send(block, block, send_ws.at[k], recv_ws.at[k], sibling).start()
    for k in range(4):
        z_from = lax.rem(z + 3 - k, 4)
        rows = pl.ds(pl.multiple_of(z_from * 128 + (1 - core) * 64, 64), 64)
        block = wo.at[pl.ds(1, 3), rows, :]
        pltpu.make_async_copy(block, block, recv_ws.at[k]).wait()

    def relay_att(q):
        pltpu.make_async_copy(att_rows(2, q), att_rows(2, q), recv_a.at[1, q]).wait()
        send(att_half(2, q, 0), att_half(3, q, 0), send_a.at[0], recv_a.at[2, q], right).start()
        pltpu.make_async_copy(att_rows(1, q), att_rows(1, q), recv_a.at[0, q]).wait()
        send(att_half(1, q, 1), att_half(3, q, 1), send_a.at[1], recv_a.at[3, q], left).start()

    def finish(q):
        for half in range(2):
            pltpu.make_async_copy(att_half(3, q, half), att_half(3, q, half), recv_a.at[2 + half, q]).wait()

        def tile(cols):
            total = jnp.dot(att[0, pl.ds(q * TQ, TQ), :], wo[0, :, cols], preferred_element_type=F32)
            for slot in range(1, 4):
                total += jnp.dot(att[slot, pl.ds(q * TQ, TQ), :], wo[slot, :, cols], preferred_element_type=F32)
            return total

        def foreign(n, carry):
            cols = pl.ds(pl.multiple_of(n * 256, 256), 256)
            pf[pl.ds(q * TQ, TQ), cols] = tile(cols).astype(BF16)
            return carry

        def mine(n, carry):
            cols = pl.ds(pl.multiple_of(n * 256, 256), 256)
            own[pl.ds(q * TQ, TQ), cols] = tile(pl.ds(pl.multiple_of(FEATS + n * 256, 256), 256))
            return carry

        lax.fori_loop(0, 4, foreign, 0)
        send(
            pf.at[pl.ds(q * TQ, TQ)], rb.at[pl.ds(q * TQ, TQ)], send_y, recv_y.at[q], opposite
        ).start()
        lax.fori_loop(0, 4, mine, 0)

    relay_att(0)
    for q in range(N_Q):
        if q + 1 < N_Q:
            relay_att(q + 1)
        finish(q)
    for q in range(N_Q):
        rows = pl.ds(q * TQ, TQ)
        pltpu.make_async_copy(rb.at[rows], rb.at[rows], recv_y.at[q]).wait()
        out[rows, :] = (own[rows, :] + rb[rows, :].astype(F32)).astype(BF16)

    for tree in range(3):
        half = pl.ds(0, TREE_STEPS[tree] * CHUNK)
        for dim in range(3):
            if MASKS[tree][dim]:

                @pl.when(sends_tree[tree][dim])
                def _(half=half, dim=dim):
                    pltpu.make_async_copy(w.at[half], w.at[half], send_w.at[dim]).wait()

    @pl.when(is_source)
    def _():
        pltpu.make_async_copy(w, w, send_sib).wait()

    @pl.when(jnp.logical_not(source_chip))
    def _():
        half = w.at[pl.ds(0, D // 2)]
        pltpu.make_async_copy(half, half, send_sib).wait()

    for side in range(2):
        pltpu.make_async_copy(xs.at[pl.ds(0, 3)], xs.at[pl.ds(0, 3)], send_x.at[side]).wait()
    pltpu.make_async_copy(xs.at[0], xs.at[0], send_x.at[2]).wait()
    pltpu.make_async_copy(sums.at[pl.ds(0, 7)], sums.at[pl.ds(0, 7)], send_s).wait()
    for slot in range(3):
        for part in range(2):
            dst = wo.at[0, pl.ds(0, 64), pl.ds(0, FEATS)]
            pltpu.make_async_copy(dst, dst, send_wx.at[slot, part]).wait()
    block = wo.at[pl.ds(1, 3), pl.ds(0, 64), :]
    for k in range(3):
        pltpu.make_async_copy(block, block, send_wz.at[k]).wait()
    for k in range(4):
        pltpu.make_async_copy(block, block, send_ws.at[k]).wait()
    for side in range(2):
        sent = att.at[0, :, :]
        pltpu.make_async_copy(sent, sent, send_a.at[side]).wait()
        sent = att.at[0, pl.ds(0, ROWS // 2)]
        pltpu.make_async_copy(sent, sent, send_a.at[side]).wait()
    pltpu.make_async_copy(pf, pf, send_y).wait()


def local(hidden_rows, lengths, attn_gain, w_joined, w_out):
    tp = lax.axis_index("tp")
    gain = lax.dynamic_slice(attn_gain, (tp * FEATS,), (FEATS,)).reshape(1, FEATS)
    dma = pltpu.SemaphoreType.DMA
    vmem = pl.BlockSpec(memory_space=pltpu.VMEM)
    anywhere = pl.BlockSpec(memory_space=pl.ANY)
    return pl.pallas_call(
        body,
        out_shape=jax.ShapeDtypeStruct((ROWS, FEATS), BF16),
        in_specs=[vmem, pl.BlockSpec(memory_space=pltpu.SMEM), vmem, anywhere, anywhere],
        out_specs=vmem,
        scratch_shapes=[
            pltpu.VMEM((D, COLS), BF16),
            pltpu.VMEM((8, ROWS, FEATS), BF16),
            pltpu.VMEM((4, ATT_COLS, 2 * FEATS), BF16),
            pltpu.VMEM((ROWS, COLS), F32),
            pltpu.VMEM((4, ROWS, ATT_COLS), BF16),
            pltpu.VMEM((ROWS, FEATS), BF16),
            pltpu.VMEM((ROWS, FEATS), BF16),
            pltpu.VMEM((ROWS, FEATS), F32),
            pltpu.VMEM((N_TP, 8, 128), F32),
            pltpu.VMEM((ROWS, 128), F32),
            pltpu.VMEM((ROWS, HD), F32),
            pltpu.VMEM((ROWS, HD), F32),
            pltpu.VMEM((HEADS, ROWS, HD), BF16),
            pltpu.VMEM((ROWS, HD), BF16),
            pltpu.VMEM((ROWS, HD), BF16),
            dma((3, max(TREE_STEPS), 2)),
            dma((3,)),
            dma,
            dma((8, N_PIECES)),
            dma((3,)),
            dma((N_TP,)),
            dma,
            dma((3, 2)),
            dma((3, 2)),
            dma((3,)),
            dma((3,)),
            dma((4,)),
            dma((4,)),
            dma((2,)),
            dma((4, N_Q)),
            dma((2,)),
            dma((N_Q,)),
            dma,
        ],
        compiler_params=pltpu.CompilerParams(
            collective_id=0, has_side_effects=True, vmem_limit_bytes=56 * 1024 * 1024
        ),
    )(hidden_rows, lengths, gain, w_joined, w_out)


def solution(mesh):
    return jax.shard_map(
        local,
        mesh=mesh,
        in_specs=(P("inst", "tp"), P("inst", None), P(), P("inst", None, "tp"), P("tp", None)),
        out_specs=P("inst", "tp"),
        check_vma=False,
    )
```

time: 381 us -> 162 us (0.43)
  waiting for transfers between devices: 325 us -> 0 us
  Pallas kernels: 0 us -> 157 us
  matrix products: 22.5 us -> 0 us
  between operations: 15 us -> 0.01 us
  other arithmetic: 14.8 us -> 0 us
    pallas_call x0 -> x1, Pallas kernels: none -> 157 us  [local(): pl.pallas_call(body, out_shape=jax.ShapeDtypeStruct((ROWS, FEATS), BF16),...]
    reduce_scatter x1 -> x0, waiting for transfers between devices: 115 us -> none  [local(): lax.psum_scatter(partial_out, 'tp', scatter_dimension=1, tiled=True)]
    all_gather x1 -> x0, waiting for transfers between devices: 106 us -> none  [local(): gathered = lax.all_gather(hidden_rows, 'tp', axis=1, tiled=True)]
    psum x1 -> x0, waiting for transfers between devices: 103 us -> none  [spread(): return lax.psum(kept, axis)]
    dot_general x4 -> x0, matrix products: 22.5 us -> none  [the longest x1 12.1 us: local(): jnp.dot(scaled, joined_weight, preferred_element_type=jnp.float32)]
    reduce_sum x4 -> x0, other arithmetic: 6.36 us -> none  [the longest x1 5.26 us: local(): jnp.mean(gathered_wide * gathered_wide, axis=1, keepdims=True) + EPSILON]
    squeeze x1 -> x0, other arithmetic: 5.58 us -> none  [local(): joined_weight = spread(w_joined, 'inst', 0)[0]]
  transfers between devices with their start and end apart: 3 -> 0, of which waited for: 3 -> 0; matrix products, arithmetic and copies ran while one was open for 3% -> 0% of each run, Pallas kernels for 0% -> 0%
where the time goes in v1:
time: 162 us; the launch traced here: 160 us
  Pallas kernels  157 us (97%)
  local copies, waits for them, and re-layouts  3.54 us (2%)
    pallas_call x1, Pallas kernels, local(): pl.pallas_call(body, out_shape=jax.ShapeDtypeStruct((ROWS, FEATS), BF16),...  157 us

profile of v1, /device:TPU:1, one launch (start us, length us, event | category | flops | bytes accessed | tf_op | source)
XLA Modules:
  0.0 160.3 jit_solution(16160339261577882963)
XLA Ops:
  0.0 1.3 dynamic_slice.3
  1.3 156.8 %shard_map.55 = bf16[512,1024]{1,0:T(8,128)(2,1)} custom-call(bf16[512,1024]{1,0:T(8,128)(2,1)} %hidden.1, s32[1,4]{1,0:T(1,128)} %lengths.1, f32[1,1024]{1,0:T(1,128)} %bitcast.1, bf16[1,8192,768]{2,1,0:T(8,128)(2,1)} %w_in.1, bf16[512,8192]{1,0:T(8,128)(2,1)} %wo_in.1), custom_call_target="tpu_custom_call" | custom-call | tf_op jit(solution)/shard_map/pallas_call | solution.py:477
  158.0 2.3 %copy.7 = bf16[512,1024]{1,0:T(8,128)(2,1)} copy(bf16[512,1024]{1,0:T(8,128)(2,1)} %shard_map.55) | data formatting | bytes 2097152

commit v2 on v1

--- a/solution.py
+++ b/solution.py
@@ -31,13 +31,15 @@
 HIGH_FACTOR = 4.0
 OLD_CONTEXT = 8192.0
 
-CHUNK = 32
-TREE_STEPS = (43, 43, 42)
-TREE_BASE = (0, 2752, 5504)
+CHUNK = 64
+TREE_STEPS = (44, 44, 40)
+TREE_BASE = (0, 2816, 5632)
 GRAY = (0, 1, 3, 2)
 LAG = 4
+AHEAD = 4
 N_SLOTS = max(TREE_STEPS) + 4 * LAG
 
+Y_FIRST = (0, 1)
 PIECE = 128
 N_PIECES = ROWS // PIECE
 TQ = 128
@@ -57,7 +59,8 @@
         for code, dim in first_edges:
             depth[code ^ (1 << dim)] = depth[code] + 1
             turned = ((code << tree) | (code >> (3 - tree))) & 7
-            masks[tree][(dim + tree) % 3] |= 1 << node_of[turned]
+            if code:
+                masks[tree][(dim + tree) % 3] |= 1 << node_of[turned]
         for code, far in depth.items():
             turned = ((code << tree) | (code >> (3 - tree))) & 7
             depths[tree] |= far << (3 * node_of[turned])
@@ -84,8 +87,8 @@
 
 def body(
     hidden, lengths, gain, w_in, wo_in, out,
-    w, xs, wo, acc, att, pf, rb, own, sums, inv, cosine, sine, qb, kb, vb,
-    recv_w, send_w, send_sib, recv_x, send_x, recv_s, send_s,
+    w, xs, xl, wo, acc, att, pf, rb, own, sums, inv, cosine, sine, qb, kb, vb,
+    recv_w, send_w, send_r, send_sib, recv_x, recv_l, send_x, recv_s, send_s,
     recv_wx, send_wx, recv_wz, send_wz, recv_ws, send_ws, loc_wo,
     recv_a, send_a, recv_y, send_y,
 ):
@@ -100,11 +103,17 @@
     def inst_of(y_lo_, z_, core_):
         return (y_lo_ * 4 + z_) * 2 + core_
 
-    right = (inst, y_hi * 4 + lax.rem(x + 1, 4))
-    left = (inst, y_hi * 4 + lax.rem(x + 3, 4))
-    across = (inst, y_hi * 4 + lax.rem(x + 2, 4))
-    opposite = (inst, (1 - y_hi) * 4 + x)
-    sibling = (inst_of(y_lo, z, 1 - core), tp)
+    tp_right = y_hi * 4 + lax.rem(x + 1, 4)
+    tp_left = y_hi * 4 + lax.rem(x + 3, 4)
+    right = (inst, tp_right)
+    left = (inst, tp_left)
+    tp_opposite = (1 - y_hi) * 4 + x
+    opposite = (inst, tp_opposite)
+    other_inst = inst_of(y_lo, z, 1 - core)
+    sibling = (other_inst, tp)
+    right_other = (other_inst, tp_right)
+    left_other = (other_inst, tp_left)
+    across_other = (other_inst, y_hi * 4 + lax.rem(x + 2, 4))
     dims = (
         (inst_of(y_lo, z + 1 - 2 * lax.rem(z, 2), core), tp),
         (inst_of(y_lo, 3 - z, core), tp),
@@ -114,19 +123,21 @@
     node = y_lo * 4 + z
     source_chip = node == 0
     is_source = jnp.logical_and(source_chip, core == 0)
+    relays_w = core == 0
+    relays_x = core == 1
 
     def send(src, dst, s_sem, r_sem, to):
         return pltpu.make_async_remote_copy(
             src_ref=src, dst_ref=dst, send_sem=s_sem, recv_sem=r_sem, device_id=to, device_id_type=MESH
         )
 
-    def chunk(tree, step, parity):
-        at = TREE_BASE[tree] + (2 * step + parity) * CHUNK
+    def chunk(tree, step):
+        at = TREE_BASE[tree] + step * CHUNK
         return pl.ds(pl.multiple_of(at, CHUNK), CHUNK)
 
     barrier = pltpu.get_barrier_semaphore()
     peers = [(inst, lax.rem(tp + k, N_TP)) for k in range(1, N_TP)]
-    greeted = peers + z_others + [sibling, dims[2]]
+    greeted = peers + z_others + [sibling, dims[2], right_other, left_other, across_other]
     for other in greeted:
         pl.semaphore_signal(barrier, inc=1, device_id=other, device_id_type=MESH)
 
@@ -135,11 +146,8 @@
         for tree in range(3):
 
             def load(step, carry, tree=tree):
-                for parity in range(2):
-                    rows = chunk(tree, step, parity)
-                    pltpu.make_async_copy(
-                        w_in.at[0, rows], w.at[rows], recv_w.at[tree, step, parity]
-                    ).start()
+                rows = chunk(tree, step)
+                pltpu.make_async_copy(w_in.at[0, rows], w.at[rows], recv_w.at[tree, step]).start()
                 return carry
 
             lax.fori_loop(0, TREE_STEPS[tree], load, 0)
@@ -159,7 +167,7 @@
     sums[tp] = jnp.zeros((8, 128), F32)
     for g in range(4):
         wide = hidden[pl.ds(g * 128, 128), :].astype(F32)
-        xs[0, pl.ds(g * 128, 128), :] = (wide * gain[...]).astype(BF16)
+        xs[0, pl.ds(g * 128, 128), :] = (wide * gain[pl.ds(tp, 1), :]).astype(BF16)
         column = jnp.sum(wide * wide, axis=1, keepdims=True)
         sums[tp, pl.ds(g, 1), :] = jnp.sum(column * eye, axis=0, keepdims=True)
 
@@ -168,108 +176,163 @@
     def piece(slot, p):
         return xs.at[slot, pl.ds(p * PIECE, PIECE)]
 
-    def send_piece(src_slot, dst_slot, p, sem, to):
-        send(piece(src_slot, p), piece(dst_slot, p), send_x.at[sem], recv_x.at[dst_slot, p], to).start()
+    def landed(block, p):
+        return xl.at[block, pl.ds(p * PIECE, PIECE)]
+
+    def send_piece(src, dst, sem, r_sem, to):
+        send(src, dst, send_x.at[sem], r_sem, to).start()
 
     def wait_piece(slot, p):
         pltpu.make_async_copy(piece(slot, p), piece(slot, p), recv_x.at[slot, p]).wait()
 
-    for p in range(N_PIECES):
-        send_piece(0, 4, p, 2, opposite)
-        send_piece(0, 2, p, 0, right)
-        send_piece(0, 1, p, 1, left)
+    def wait_landed(block, p):
+        pltpu.make_async_copy(landed(block, p), landed(block, p), recv_l.at[block, p]).wait()
+
+    def to_final(src, slot, p, sem, to):
+        send_piece(src, piece(slot, p), sem, recv_x.at[slot, p], to)
+
+    def to_relay(src, block, p, sem, to):
+        send_piece(src, landed(block, p), sem, recv_l.at[block, p], to)
+
+    def cross(p):
+        to_final(piece(0, p), 4, p, 2, opposite)
+        to_relay(landed(3, p), 1, p, 2, opposite)
+
+    @pl.when(relays_w)
+    def _():
+        for p in range(N_PIECES):
+            to_relay(piece(0, p), 3, p, 2, sibling)
+
+    @pl.when(relays_x)
+    def _():
+        for p in range(N_PIECES):
+            to_final(piece(0, p), 2, p, 0, right)
+            to_final(piece(0, p), 1, p, 1, left)
+            wait_landed(3, p)
+            if p % 2 == 0:
+                to_relay(landed(3, p), 0, p, 0, right)
+                to_final(landed(3, p), 1, p, 1, left_other)
+            else:
+                to_final(landed(3, p), 2, p, 0, right_other)
+                to_relay(landed(3, p), 0, p, 1, left)
+            if p in Y_FIRST:
+                cross(p)
+
     for other in peers:
         send(sums.at[tp], sums.at[tp], send_s, recv_s.at[tp], other).start()
 
-    wo_rows = pl.ds(pl.multiple_of(z * 128 + core * 64, 64), 64)
-    wo_targets = ((2, right, 1), (1, left, 3), (3, across, 2))
-    for slot, to, shift in wo_targets:
-        x_to = lax.rem(x + shift, 4)
-        for part, y_part in ((0, 1 - y_hi), (1, y_hi)):
-            cols = pl.ds(pl.multiple_of((y_part * 4 + x_to) * FEATS, FEATS), FEATS)
-            send(
-                wo_in.at[wo_rows, cols],
-                wo.at[slot, wo_rows, pl.ds(part * FEATS, FEATS)],
-                send_wx.at[slot - 1, part],
-                recv_wx.at[slot - 1, part],
-                to,
-            ).start()
+    wo_rows = pl.ds(pl.multiple_of(z * 128, 128), 128)
+    wo_targets = ((2, right_other, 1), (1, left_other, 3), (3, across_other, 2))
+
+    def wo_sends():
+        for slot, to, shift in wo_targets:
+            x_to = lax.rem(x + shift, 4)
+            for part, y_part in ((0, 1 - y_hi), (1, y_hi)):
+                cols = pl.ds(pl.multiple_of((y_part * 4 + x_to) * FEATS, FEATS), FEATS)
+                send(
+                    wo_in.at[wo_rows, cols],
+                    wo.at[slot, wo_rows, pl.ds(part * FEATS, FEATS)],
+                    send_wx.at[slot - 1, part],
+                    recv_wx.at[slot - 1, part],
+                    to,
+                ).start()
 
     sends_tree = [
         [((MASKS[tree][dim] >> node) & 1) == 1 for dim in range(3)] for tree in range(3)
     ]
 
     def weight_tree(tree, step):
-        mine = chunk(tree, step, core)
-        pltpu.make_async_copy(w.at[mine], w.at[mine], recv_w.at[tree, step, core]).wait()
+        rows = chunk(tree, step)
+        pltpu.make_async_copy(w.at[rows], w.at[rows], recv_w.at[tree, step]).wait()
         for dim in range(3):
             if MASKS[tree][dim]:
 
                 @pl.when(sends_tree[tree][dim])
                 def _(dim=dim):
-                    send(w.at[mine], w.at[mine], send_w.at[dim], recv_w.at[tree, step, core], dims[dim]).start()
-
-        @pl.when(jnp.logical_or(jnp.logical_not(source_chip), core == 0))
-        def _():
-            send(w.at[mine], w.at[mine], send_sib, recv_w.at[tree, step, core], sibling).start()
+                    send(w.at[rows], w.at[rows], send_w.at[dim], recv_w.at[tree, step], dims[dim]).start()
 
         @pl.when(is_source)
         def _():
-            theirs = chunk(tree, step, 1)
-            pltpu.make_async_copy(w.at[theirs], w.at[theirs], recv_w.at[tree, step, 1]).wait()
-            send(w.at[theirs], w.at[theirs], send_sib, recv_w.at[tree, step, 1], sibling).start()
-
-    def weight_steps(low, high):
-        def slot_of(slot, carry):
-            for tree in range(3):
-                step = slot - LAG * ((DEPTHS[tree] >> (3 * node)) & 7)
-
-                @pl.when(jnp.logical_and(step >= 0, step < TREE_STEPS[tree]))
-                def _(tree=tree, step=step):
-                    weight_tree(tree, step)
-
-            return carry
-
-        lax.fori_loop(low, high, slot_of, 0)
-
-    def relay_ring(h, e):
-        wait_piece(4 * h + 2, e)
-        send_piece(4 * h + 2, 4 * h + 3, e, 0, right)
-        wait_piece(4 * h + 1, 2 + e)
-        send_piece(4 * h + 1, 4 * h + 3, 2 + e, 1, left)
-
-    def relay_opposite(p):
-        wait_piece(4, p)
-        send_piece(4, 6, p, 0, right)
-        send_piece(4, 5, p, 1, left)
-
-    def wo_spread():
+            turn = lax.rem(step, AHEAD)
+
+            @pl.when(step >= AHEAD)
+            def _():
+                pltpu.make_async_copy(w.at[rows], w.at[rows], send_r.at[tree, turn]).wait()
+
+            send(w.at[rows], w.at[rows], send_r.at[tree, turn], recv_w.at[tree, step], dims[tree]).start()
+
+        send(w.at[rows], w.at[rows], send_sib, recv_w.at[tree, step], sibling).start()
+
+    def wo_arrived():
         for slot in range(3):
             for part in range(2):
                 dst = wo.at[slot + 1, wo_rows, pl.ds(part * FEATS, FEATS)]
                 pltpu.make_async_copy(dst, dst, recv_wx.at[slot, part]).wait()
         block = wo.at[pl.ds(1, 3), wo_rows, :]
+        send(block, block, send_ws.at[3], recv_ws.at[3], sibling).start()
+
         for k, to in enumerate(z_others):
             send(block, block, send_wz.at[k], recv_wz.at[k], to).start()
-        send(block, block, send_ws.at[3], recv_ws.at[3], sibling).start()
-
-    weight_steps(0, 22)
-    relay_ring(0, 0)
-    relay_ring(0, 1)
-    weight_steps(22, 28)
-    relay_opposite(0)
-    weight_steps(28, 32)
-    relay_opposite(1)
-    weight_steps(32, 36)
-    relay_opposite(2)
-    weight_steps(36, 40)
-    relay_opposite(3)
-    weight_steps(40, 48)
-    relay_ring(1, 0)
-    weight_steps(48, 52)
-    relay_ring(1, 1)
-    weight_steps(52, N_SLOTS)
-    wo_spread()
+
+    def weight_steps():
+        def slot_of(slot, carry):
+            for tree in range(3):
+                step = slot - LAG * ((DEPTHS[tree] >> (3 * node)) & 7)
+
+                @pl.when(jnp.logical_and(step >= 0, step < TREE_STEPS[tree]))
+                def _(tree=tree, step=step):
+                    weight_tree(tree, step)
+
+            return carry
+
+        lax.fori_loop(0, N_SLOTS, slot_of, 0)
+
+    def relay_ring(h, e):
+        p = 2 * e
+        wait_piece(4 * h + 2, p)
+        to_final(piece(4 * h + 2, p), 4 * h + 3, p, 0, right)
+        wait_landed(2 * h, p)
+        to_final(landed(2 * h, p), 4 * h + 3, p, 0, right_other)
+        to_final(landed(2 * h, p), 4 * h + 2, p, 3, sibling)
+        p = 2 * e + 1
+        wait_piece(4 * h + 1, p)
+        to_final(piece(4 * h + 1, p), 4 * h + 3, p, 1, left)
+        wait_landed(2 * h, p)
+        to_final(landed(2 * h, p), 4 * h + 3, p, 1, left_other)
+        to_final(landed(2 * h, p), 4 * h + 1, p, 3, sibling)
+
+    def relay_opposite(p):
+        wait_piece(4, p)
+        to_final(piece(4, p), 6, p, 0, right)
+        to_final(piece(4, p), 5, p, 1, left)
+        wait_landed(1, p)
+        if p % 2 == 0:
+            to_relay(landed(1, p), 2, p, 0, right)
+            to_final(landed(1, p), 5, p, 1, left_other)
+        else:
+            to_final(landed(1, p), 6, p, 0, right_other)
+            to_relay(landed(1, p), 2, p, 1, left)
+        to_final(landed(1, p), 4, p, 3, sibling)
+
+    @pl.when(relays_w)
+    def _():
+        weight_steps()
+        wo_arrived()
+
+    @pl.when(relays_x)
+    def _():
+        relay_ring(0, 0)
+        relay_ring(0, 1)
+        wo_sends()
+        relay_opposite(0)
+        relay_opposite(1)
+        relay_ring(1, 0)
+        for p in range(N_PIECES):
+            if p not in Y_FIRST:
+                cross(p)
+        relay_opposite(2)
+        relay_opposite(3)
+        relay_ring(1, 1)
 
     length = [lengths[0, k] for k in range(3)]
     begins = [length[0], length[0] + length[1], length[0] + length[1] + length[2]]
@@ -282,17 +345,16 @@
 
     cosine[...], sine[...] = rope_tables(start_of, ROWS)
 
-    for tree in range(3):
-
-        def others(step, carry, tree=tree):
-            @pl.when(jnp.logical_not(is_source))
-            def _():
-                theirs = chunk(tree, step, 1 - core)
-                pltpu.make_async_copy(w.at[theirs], w.at[theirs], recv_w.at[tree, step, 1 - core]).wait()
-
-            return carry
-
-        lax.fori_loop(0, TREE_STEPS[tree], others, 0)
+    @pl.when(relays_x)
+    def _():
+        for tree in range(3):
+
+            def passed(step, carry, tree=tree):
+                rows = chunk(tree, step)
+                pltpu.make_async_copy(w.at[rows], w.at[rows], recv_w.at[tree, step]).wait()
+                return carry
+
+            lax.fori_loop(0, TREE_STEPS[tree], passed, 0)
 
     acc[...] = jnp.zeros_like(acc)
 
@@ -301,7 +363,8 @@
         h = slot // 4
 
         for p in range(N_PIECES):
-            seen = (turn == 0) | ((turn == 2) & (p < 2)) | ((turn == 1) & (p >= 2))
+            relayed = (turn == 0) | ((turn == 2) & (p % 2 == 0)) | ((turn == 1) & (p % 2 == 1))
+            seen = (slot == 0) | (relays_x & relayed)
 
             @pl.when(jnp.logical_not(seen))
             def _(p=p):
@@ -350,6 +413,12 @@
 
     def att_half(slot, q, half):
         return att.at[slot, pl.ds(q * TQ + half * (TQ // 2), TQ // 2)]
+
+    def wo_pass(k):
+        z_from = lax.rem(z + 3 - k, 4)
+        block = wo.at[pl.ds(1, 3), pl.ds(pl.multiple_of(z_from * 128, 128), 128), :]
+        pltpu.make_async_copy(block, block, recv_wz.at[k]).wait()
+        send(block, block, send_ws.at[k], recv_ws.at[k], sibling).start()
 
     for q in range(N_Q):
         low = max(0, q * TQ - LONGEST)
@@ -373,19 +442,19 @@
         send(att_rows(0, q), att_rows(2, q), send_a.at[0], recv_a.at[1, q], right).start()
         send(att_rows(0, q), att_rows(1, q), send_a.at[1], recv_a.at[0, q], left).start()
 
+    @pl.when(relays_w)
+    def _():
+        for k in (0, 2, 1):
+            wo_pass(k)
+
     for copy in wo_local:
         copy.wait()
-    for k in range(3):
-        z_from = lax.rem(z + 3 - k, 4)
-        rows = pl.ds(pl.multiple_of(z_from * 128 + core * 64, 64), 64)
-        block = wo.at[pl.ds(1, 3), rows, :]
-        pltpu.make_async_copy(block, block, recv_wz.at[k]).wait()
-        send(block, block, send_ws.at[k], recv_ws.at[k], sibling).start()
-    for k in range(4):
-        z_from = lax.rem(z + 3 - k, 4)
-        rows = pl.ds(pl.multiple_of(z_from * 128 + (1 - core) * 64, 64), 64)
-        block = wo.at[pl.ds(1, 3), rows, :]
-        pltpu.make_async_copy(block, block, recv_ws.at[k]).wait()
+    @pl.when(relays_x)
+    def _():
+        for k in range(4):
+            z_from = lax.rem(z + 3 - k, 4)
+            block = wo.at[pl.ds(1, 3), pl.ds(pl.multiple_of(z_from * 128, 128), 128), :]
+            pltpu.make_async_copy(block, block, recv_ws.at[k]).wait()
 
     def relay_att(q):
         pltpu.make_async_copy(att_rows(2, q), att_rows(2, q), recv_a.at[1, q]).wait()
@@ -429,48 +498,52 @@
         pltpu.make_async_copy(rb.at[rows], rb.at[rows], recv_y.at[q]).wait()
         out[rows, :] = (own[rows, :] + rb[rows, :].astype(F32)).astype(BF16)
 
-    for tree in range(3):
-        half = pl.ds(0, TREE_STEPS[tree] * CHUNK)
-        for dim in range(3):
-            if MASKS[tree][dim]:
-
-                @pl.when(sends_tree[tree][dim])
-                def _(half=half, dim=dim):
-                    pltpu.make_async_copy(w.at[half], w.at[half], send_w.at[dim]).wait()
-
-    @pl.when(is_source)
-    def _():
-        pltpu.make_async_copy(w, w, send_sib).wait()
-
-    @pl.when(jnp.logical_not(source_chip))
-    def _():
-        half = w.at[pl.ds(0, D // 2)]
-        pltpu.make_async_copy(half, half, send_sib).wait()
-
+    def sent(ref, sem):
+        pltpu.make_async_copy(ref, ref, sem).wait()
+
+    @pl.when(relays_w)
+    def _():
+        for tree in range(3):
+            for dim in range(3):
+                if MASKS[tree][dim]:
+
+                    @pl.when(sends_tree[tree][dim])
+                    def _(tree=tree, dim=dim):
+                        sent(w.at[pl.ds(0, TREE_STEPS[tree] * CHUNK)], send_w.at[dim])
+
+        @pl.when(is_source)
+        def _():
+            for tree in range(3):
+                for turn in range(AHEAD):
+                    sent(w.at[pl.ds(0, CHUNK)], send_r.at[tree, turn])
+
+        sent(w, send_sib)
+        sent(xs.at[0], send_x.at[2])
+        block = wo.at[pl.ds(1, 3), pl.ds(0, 128), :]
+        for k in range(3):
+            sent(block, send_wz.at[k])
+        for k in range(4):
+            sent(block, send_ws.at[k])
+
+    @pl.when(relays_x)
+    def _():
+        for side in range(2):
+            sent(xs.at[pl.ds(0, 6)], send_x.at[side])
+        sent(xs.at[pl.ds(0, 2)], send_x.at[2])
+        sent(xs.at[pl.ds(0, 3)], send_x.at[3])
+        for slot in range(3):
+            for part in range(2):
+                sent(wo.at[0, pl.ds(0, 128), pl.ds(0, FEATS)], send_wx.at[slot, part])
+
+    sent(sums.at[pl.ds(0, 7)], send_s)
     for side in range(2):
-        pltpu.make_async_copy(xs.at[pl.ds(0, 3)], xs.at[pl.ds(0, 3)], send_x.at[side]).wait()
-    pltpu.make_async_copy(xs.at[0], xs.at[0], send_x.at[2]).wait()
-    pltpu.make_async_copy(sums.at[pl.ds(0, 7)], sums.at[pl.ds(0, 7)], send_s).wait()
-    for slot in range(3):
-        for part in range(2):
-            dst = wo.at[0, pl.ds(0, 64), pl.ds(0, FEATS)]
-            pltpu.make_async_copy(dst, dst, send_wx.at[slot, part]).wait()
-    block = wo.at[pl.ds(1, 3), pl.ds(0, 64), :]
-    for k in range(3):
-        pltpu.make_async_copy(block, block, send_wz.at[k]).wait()
-    for k in range(4):
-        pltpu.make_async_copy(block, block, send_ws.at[k]).wait()
-    for side in range(2):
-        sent = att.at[0, :, :]
-        pltpu.make_async_copy(sent, sent, send_a.at[side]).wait()
-        sent = att.at[0, pl.ds(0, ROWS // 2)]
-        pltpu.make_async_copy(sent, sent, send_a.at[side]).wait()
-    pltpu.make_async_copy(pf, pf, send_y).wait()
+        sent(att.at[0], send_a.at[side])
+        sent(att.at[0, pl.ds(0, ROWS // 2)], send_a.at[side])
+    sent(pf, send_y)
 
 
 def local(hidden_rows, lengths, attn_gain, w_joined, w_out):
-    tp = lax.axis_index("tp")
-    gain = lax.dynamic_slice(attn_gain, (tp * FEATS,), (FEATS,)).reshape(1, FEATS)
+    gain = attn_gain.reshape(N_TP, FEATS)
     dma = pltpu.SemaphoreType.DMA
     vmem = pl.BlockSpec(memory_space=pltpu.VMEM)
     anywhere = pl.BlockSpec(memory_space=pl.ANY)
@@ -482,6 +555,7 @@
         scratch_shapes=[
             pltpu.VMEM((D, COLS), BF16),
             pltpu.VMEM((8, ROWS, FEATS), BF16),
+            pltpu.VMEM((4, ROWS, FEATS), BF16),
             pltpu.VMEM((4, ATT_COLS, 2 * FEATS), BF16),
             pltpu.VMEM((ROWS, COLS), F32),
             pltpu.VMEM((4, ROWS, ATT_COLS), BF16),
@@ -495,11 +569,13 @@
             pltpu.VMEM((HEADS, ROWS, HD), BF16),
             pltpu.VMEM((ROWS, HD), BF16),
             pltpu.VMEM((ROWS, HD), BF16),
-            dma((3, max(TREE_STEPS), 2)),
+            dma((3, max(TREE_STEPS))),
             dma((3,)),
+            dma((3, AHEAD)),
             dma,
             dma((8, N_PIECES)),
-            dma((3,)),
+            dma((4, N_PIECES)),
+            dma((4,)),
             dma((N_TP,)),
             dma,
             dma((3, 2)),

time: 162 us -> 158 us (0.975)
  Pallas kernels: 157 us -> 154 us
    pallas_call x1, Pallas kernels: 157 us -> 154 us  [local(): pl.pallas_call(body, out_shape=jax.ShapeDtypeStruct((ROWS, FEATS), BF16),...]
where the time goes in v2:
time: 158 us
  Pallas kernels  154 us (97%)
  local copies, waits for them, and re-layouts  3.65 us (2%)
    pallas_call x1, Pallas kernels, local(): pl.pallas_call(body, out_shape=jax.ShapeDtypeStruct((ROWS, FEATS), BF16),...  154 us

profile of v2, /device:TPU:1, one launch (start us, length us, event | category | flops | bytes accessed | tf_op | source)
XLA Modules:
  0.0 157.6 jit_solution(8634100579027817614)
XLA Ops:
  0.0 1.4 reshape.3.gain
  1.4 154.0 %shard_map.55 = bf16[512,1024]{1,0:T(8,128)(2,1)} custom-call(bf16[512,1024]{1,0:T(8,128)(2,1)} %hidden.1, s32[1,4]{1,0:T(1,128)} %lengths.1, f32[8,1024]{1,0:T(8,128)} %reshape.3.gain, bf16[1,8192,768]{2,1,0:T(8,128)(2,1)} %w_in.1, bf16[512,8192]{1,0:T(8,128)(2,1)} %wo_in.1), custom_call_target="tpu_custom_call" | custom-call | tf_op jit(solution)/shard_map/pallas_call | solution.py:550
  155.3 2.3 %copy.7 = bf16[512,1024]{1,0:T(8,128)(2,1)} copy(bf16[512,1024]{1,0:T(8,128)(2,1)} %shard_map.55) | data formatting | bytes 2097152

commit v3 on v2

--- a/solution.py
+++ b/solution.py
@@ -39,7 +39,7 @@
 AHEAD = 4
 N_SLOTS = max(TREE_STEPS) + 4 * LAG
 
-Y_FIRST = (0, 1)
+Y_FIRST = (0, 1, 2)
 PIECE = 128
 N_PIECES = ROWS // PIECE
 TQ = 128
@@ -165,9 +165,10 @@
         lax.broadcasted_iota(jnp.int32, (128, 128), 0) == lax.broadcasted_iota(jnp.int32, (128, 128), 1)
     ).astype(F32)
     sums[tp] = jnp.zeros((8, 128), F32)
+    gain_row = gain[pl.ds(pl.multiple_of(tp * FEATS, FEATS), FEATS)].reshape(1, FEATS)
     for g in range(4):
         wide = hidden[pl.ds(g * 128, 128), :].astype(F32)
-        xs[0, pl.ds(g * 128, 128), :] = (wide * gain[pl.ds(tp, 1), :]).astype(BF16)
+        xs[0, pl.ds(g * 128, 128), :] = (wide * gain_row).astype(BF16)
         column = jnp.sum(wide * wide, axis=1, keepdims=True)
         sums[tp, pl.ds(g, 1), :] = jnp.sum(column * eye, axis=0, keepdims=True)
 
@@ -221,19 +222,22 @@
     for other in peers:
         send(sums.at[tp], sums.at[tp], send_s, recv_s.at[tp], other).start()
 
-    wo_rows = pl.ds(pl.multiple_of(z * 128, 128), 128)
+    def wo_block(quarter):
+        return wo.at[pl.ds(1, 3), pl.ds(pl.multiple_of(lax.rem(z + quarter, 4) * 128, 128), 128), :]
+
     wo_targets = ((2, right_other, 1), (1, left_other, 3), (3, across_other, 2))
 
-    def wo_sends():
+    def wo_sends(turn):
+        rows = pl.ds(pl.multiple_of(lax.rem(z + 2 * turn, 4) * 128, 128), 128)
         for slot, to, shift in wo_targets:
             x_to = lax.rem(x + shift, 4)
             for part, y_part in ((0, 1 - y_hi), (1, y_hi)):
                 cols = pl.ds(pl.multiple_of((y_part * 4 + x_to) * FEATS, FEATS), FEATS)
                 send(
-                    wo_in.at[wo_rows, cols],
-                    wo.at[slot, wo_rows, pl.ds(part * FEATS, FEATS)],
-                    send_wx.at[slot - 1, part],
-                    recv_wx.at[slot - 1, part],
+                    wo_in.at[rows, cols],
+                    wo.at[slot, rows, pl.ds(part * FEATS, FEATS)],
+                    send_wx.at[turn, slot - 1, part],
+                    recv_wx.at[turn, slot - 1, part],
                     to,
                 ).start()
 
@@ -263,16 +267,29 @@
 
         send(w.at[rows], w.at[rows], send_sib, recv_w.at[tree, step], sibling).start()
 
-    def wo_arrived():
+    def wo_arrived(turn):
+        rows = pl.ds(pl.multiple_of(lax.rem(z + 2 * turn, 4) * 128, 128), 128)
         for slot in range(3):
             for part in range(2):
-                dst = wo.at[slot + 1, wo_rows, pl.ds(part * FEATS, FEATS)]
-                pltpu.make_async_copy(dst, dst, recv_wx.at[slot, part]).wait()
-        block = wo.at[pl.ds(1, 3), wo_rows, :]
-        send(block, block, send_ws.at[3], recv_ws.at[3], sibling).start()
-
-        for k, to in enumerate(z_others):
+                dst = wo.at[slot + 1, rows, pl.ds(part * FEATS, FEATS)]
+                pltpu.make_async_copy(dst, dst, recv_wx.at[turn, slot, part]).wait()
+
+    def wo_to_sibling(quarter):
+        block = wo_block(quarter)
+        send(block, block, send_ws.at[quarter], recv_ws.at[quarter], sibling).start()
+
+    def wo_spread():
+        wo_arrived(0)
+        block = wo_block(0)
+        for k, to in ((0, z_others[0]), (1, z_others[2])):
             send(block, block, send_wz.at[k], recv_wz.at[k], to).start()
+        wo_to_sibling(0)
+
+    def wo_pass(k):
+        quarter = 3 - 2 * k
+        block = wo_block(quarter)
+        pltpu.make_async_copy(block, block, recv_wz.at[k]).wait()
+        wo_to_sibling(quarter)
 
     def weight_steps():
         def slot_of(slot, carry):
@@ -314,16 +331,30 @@
             to_relay(landed(1, p), 2, p, 1, left)
         to_final(landed(1, p), 4, p, 3, sibling)
 
+    length = [lengths[0, k] for k in range(3)]
+    begins = [length[0], length[0] + length[1], length[0] + length[1] + length[2]]
+
+    def start_of(row):
+        start = jnp.zeros_like(row)
+        for begin in begins:
+            start = jnp.where(row >= begin, begin, start)
+        return start
+
+    def fill_tables():
+        cosine[...], sine[...] = rope_tables(start_of, ROWS)
+
     @pl.when(relays_w)
     def _():
         weight_steps()
-        wo_arrived()
+        wo_spread()
+        fill_tables()
 
     @pl.when(relays_x)
     def _():
+        fill_tables()
         relay_ring(0, 0)
         relay_ring(0, 1)
-        wo_sends()
+        wo_sends(0)
         relay_opposite(0)
         relay_opposite(1)
         relay_ring(1, 0)
@@ -333,17 +364,7 @@
         relay_opposite(2)
         relay_opposite(3)
         relay_ring(1, 1)
-
-    length = [lengths[0, k] for k in range(3)]
-    begins = [length[0], length[0] + length[1], length[0] + length[1] + length[2]]
-
-    def start_of(row):
-        start = jnp.zeros_like(row)
-        for begin in begins:
-            start = jnp.where(row >= begin, begin, start)
-        return start
-
-    cosine[...], sine[...] = rope_tables(start_of, ROWS)
+        wo_sends(1)
 
     @pl.when(relays_x)
     def _():
@@ -413,12 +434,6 @@
 
     def att_half(slot, q, half):
         return att.at[slot, pl.ds(q * TQ + half * (TQ // 2), TQ // 2)]
-
-    def wo_pass(k):
-        z_from = lax.rem(z + 3 - k, 4)
-        block = wo.at[pl.ds(1, 3), pl.ds(pl.multiple_of(z_from * 128, 128), 128), :]
-        pltpu.make_async_copy(block, block, recv_wz.at[k]).wait()
-        send(block, block, send_ws.at[k], recv_ws.at[k], sibling).start()
 
     for q in range(N_Q):
         low = max(0, q * TQ - LONGEST)
@@ -442,19 +457,22 @@
         send(att_rows(0, q), att_rows(2, q), send_a.at[0], recv_a.at[1, q], right).start()
         send(att_rows(0, q), att_rows(1, q), send_a.at[1], recv_a.at[0, q], left).start()
 
-    @pl.when(relays_w)
-    def _():
-        for k in (0, 2, 1):
-            wo_pass(k)
+        @pl.when(relays_w)
+        def _(q=q):
+            if q in (1, 2):
+                wo_pass(q - 1)
+            elif q == 3:
+                wo_arrived(1)
+                wo_to_sibling(2)
 
     for copy in wo_local:
         copy.wait()
+
     @pl.when(relays_x)
     def _():
-        for k in range(4):
-            z_from = lax.rem(z + 3 - k, 4)
-            block = wo.at[pl.ds(1, 3), pl.ds(pl.multiple_of(z_from * 128, 128), 128), :]
-            pltpu.make_async_copy(block, block, recv_ws.at[k]).wait()
+        for quarter in range(4):
+            block = wo_block(quarter)
+            pltpu.make_async_copy(block, block, recv_ws.at[quarter]).wait()
 
     def relay_att(q):
         pltpu.make_async_copy(att_rows(2, q), att_rows(2, q), recv_a.at[1, q]).wait()
@@ -462,37 +480,40 @@
         pltpu.make_async_copy(att_rows(1, q), att_rows(1, q), recv_a.at[0, q]).wait()
         send(att_half(1, q, 1), att_half(3, q, 1), send_a.at[1], recv_a.at[3, q], left).start()
 
-    def finish(q):
+    def tile(q, cols):
+        total = jnp.dot(att[0, pl.ds(q * TQ, TQ), :], wo[0, :, cols], preferred_element_type=F32)
+        for slot in range(1, 4):
+            total += jnp.dot(att[slot, pl.ds(q * TQ, TQ), :], wo[slot, :, cols], preferred_element_type=F32)
+        return total
+
+    def foreign_part(q):
         for half in range(2):
             pltpu.make_async_copy(att_half(3, q, half), att_half(3, q, half), recv_a.at[2 + half, q]).wait()
 
-        def tile(cols):
-            total = jnp.dot(att[0, pl.ds(q * TQ, TQ), :], wo[0, :, cols], preferred_element_type=F32)
-            for slot in range(1, 4):
-                total += jnp.dot(att[slot, pl.ds(q * TQ, TQ), :], wo[slot, :, cols], preferred_element_type=F32)
-            return total
-
         def foreign(n, carry):
             cols = pl.ds(pl.multiple_of(n * 256, 256), 256)
-            pf[pl.ds(q * TQ, TQ), cols] = tile(cols).astype(BF16)
+            pf[pl.ds(q * TQ, TQ), cols] = tile(q, cols).astype(BF16)
             return carry
 
+        lax.fori_loop(0, 4, foreign, 0)
+        rows = pl.ds(q * TQ, TQ)
+        send(pf.at[rows], rb.at[rows], send_y, recv_y.at[q], opposite).start()
+
+    def own_part(q):
         def mine(n, carry):
             cols = pl.ds(pl.multiple_of(n * 256, 256), 256)
-            own[pl.ds(q * TQ, TQ), cols] = tile(pl.ds(pl.multiple_of(FEATS + n * 256, 256), 256))
+            own[pl.ds(q * TQ, TQ), cols] = tile(q, pl.ds(pl.multiple_of(FEATS + n * 256, 256), 256))
             return carry
 
-        lax.fori_loop(0, 4, foreign, 0)
-        send(
-            pf.at[pl.ds(q * TQ, TQ)], rb.at[pl.ds(q * TQ, TQ)], send_y, recv_y.at[q], opposite
-        ).start()
         lax.fori_loop(0, 4, mine, 0)
 
     relay_att(0)
     for q in range(N_Q):
         if q + 1 < N_Q:
             relay_att(q + 1)
-        finish(q)
+        foreign_part(q)
+    for q in range(N_Q):
+        own_part(q)
     for q in range(N_Q):
         rows = pl.ds(q * TQ, TQ)
         pltpu.make_async_copy(rb.at[rows], rb.at[rows], recv_y.at[q]).wait()
@@ -519,11 +540,10 @@
 
         sent(w, send_sib)
         sent(xs.at[0], send_x.at[2])
-        block = wo.at[pl.ds(1, 3), pl.ds(0, 128), :]
-        for k in range(3):
-            sent(block, send_wz.at[k])
-        for k in range(4):
-            sent(block, send_ws.at[k])
+        for k in range(2):
+            sent(wo_block(0), send_wz.at[k])
+        for quarter in range(4):
+            sent(wo_block(0), send_ws.at[quarter])
 
     @pl.when(relays_x)
     def _():
@@ -531,9 +551,10 @@
             sent(xs.at[pl.ds(0, 6)], send_x.at[side])
         sent(xs.at[pl.ds(0, 2)], send_x.at[2])
         sent(xs.at[pl.ds(0, 3)], send_x.at[3])
-        for slot in range(3):
-            for part in range(2):
-                sent(wo.at[0, pl.ds(0, 128), pl.ds(0, FEATS)], send_wx.at[slot, part])
+        for turn in range(2):
+            for slot in range(3):
+                for part in range(2):
+                    sent(wo.at[0, pl.ds(0, 128), pl.ds(0, FEATS)], send_wx.at[turn, slot, part])
 
     sent(sums.at[pl.ds(0, 7)], send_s)
     for side in range(2):
@@ -543,7 +564,6 @@
 
 
 def local(hidden_rows, lengths, attn_gain, w_joined, w_out):
-    gain = attn_gain.reshape(N_TP, FEATS)
     dma = pltpu.SemaphoreType.DMA
     vmem = pl.BlockSpec(memory_space=pltpu.VMEM)
     anywhere = pl.BlockSpec(memory_space=pl.ANY)
@@ -578,10 +598,10 @@
             dma((4,)),
             dma((N_TP,)),
             dma,
-            dma((3, 2)),
-            dma((3, 2)),
-            dma((3,)),
-            dma((3,)),
+            dma((2, 3, 2)),
+            dma((2, 3, 2)),
+            dma((2,)),
+            dma((2,)),
             dma((4,)),
             dma((4,)),
             dma((2,)),
@@ -593,7 +613,7 @@
         compiler_params=pltpu.CompilerParams(
             collective_id=0, has_side_effects=True, vmem_limit_bytes=56 * 1024 * 1024
         ),
-    )(hidden_rows, lengths, gain, w_joined, w_out)
+    )(hidden_rows, lengths, attn_gain, w_joined, w_out)
 
 
 def solution(mesh):

time: 158 us -> 148 us (0.937)
  Pallas kernels: 154 us -> 144 us
    pallas_call x1, Pallas kernels: 154 us -> 144 us  [local(): pl.pallas_call(body, out_shape=jax.ShapeDtypeStruct((ROWS, FEATS), BF16),...]
where the time goes in v3:
time: 148 us; the launch traced here: 146 us
  Pallas kernels  144 us (97%)
  local copies, waits for them, and re-layouts  2.26 us (2%)
    pallas_call x1, Pallas kernels, local(): pl.pallas_call(body, out_shape=jax.ShapeDtypeStruct((ROWS, FEATS), BF16),...  144 us

profile of v3, /device:TPU:1, one launch (start us, length us, event | category | flops | bytes accessed | tf_op | source)
XLA Modules:
  0.0 146.3 jit_solution(12324727236720868017)
XLA Ops:
  0.0 144.0 %shard_map.55 = bf16[512,1024]{1,0:T(8,128)(2,1)} custom-call(bf16[512,1024]{1,0:T(8,128)(2,1)} %hidden.1, s32[1,4]{1,0:T(1,128)} %lengths.1, f32[8192]{0:T(1024)} %gain.1, bf16[1,8192,768]{2,1,0:T(8,128)(2,1)} %w_in.1, bf16[512,8192]{1,0:T(8,128)(2,1)} %wo_in.1), custom_call_target="tpu_custom_call" | custom-call | tf_op jit(solution)/shard_map/pallas_call | solution.py:570
  144.0 2.3 %copy.7 = bf16[512,1024]{1,0:T(8,128)(2,1)} copy(bf16[512,1024]{1,0:T(8,128)(2,1)} %shard_map.55) | data formatting | bytes 2097152

commit v4 on v3

--- a/solution.py
+++ b/solution.py
@@ -459,9 +459,9 @@
 
         @pl.when(relays_w)
         def _(q=q):
-            if q in (1, 2):
-                wo_pass(q - 1)
-            elif q == 3:
+            if q == 3:
+                wo_pass(0)
+                wo_pass(1)
                 wo_arrived(1)
                 wo_to_sibling(2)
 

time: 148 us -> 147 us (level)
  no operation moved by 1% of the time
where the time goes in v4:
time: 147 us; the launch traced here: 146 us
  Pallas kernels  144 us (98%)
  local copies, waits for them, and re-layouts  2.26 us (2%)
    pallas_call x1, Pallas kernels, local(): pl.pallas_call(body, out_shape=jax.ShapeDtypeStruct((ROWS, FEATS), BF16),...  144 us

profile of v4, /device:TPU:1, one launch (start us, length us, event | category | flops | bytes accessed | tf_op | source)
XLA Modules:
  0.0 146.0 jit_solution(9794367238205460307)
XLA Ops:
  0.0 143.7 %shard_map.55 = bf16[512,1024]{1,0:T(8,128)(2,1)} custom-call(bf16[512,1024]{1,0:T(8,128)(2,1)} %hidden.1, s32[1,4]{1,0:T(1,128)} %lengths.1, f32[8192]{0:T(1024)} %gain.1, bf16[1,8192,768]{2,1,0:T(8,128)(2,1)} %w_in.1, bf16[512,8192]{1,0:T(8,128)(2,1)} %wo_in.1), custom_call_target="tpu_custom_call" | custom-call | tf_op jit(solution)/shard_map/pallas_call | solution.py:570
  143.7 2.3 %copy.7 = bf16[512,1024]{1,0:T(8,128)(2,1)} copy(bf16[512,1024]{1,0:T(8,128)(2,1)} %shard_map.55) | data formatting | bytes 2097152

commit v5 on v4

--- a/solution.py
+++ b/solution.py
@@ -164,13 +164,10 @@
     eye = (
         lax.broadcasted_iota(jnp.int32, (128, 128), 0) == lax.broadcasted_iota(jnp.int32, (128, 128), 1)
     ).astype(F32)
-    sums[tp] = jnp.zeros((8, 128), F32)
     gain_row = gain[pl.ds(pl.multiple_of(tp * FEATS, FEATS), FEATS)].reshape(1, FEATS)
     for g in range(4):
         wide = hidden[pl.ds(g * 128, 128), :].astype(F32)
         xs[0, pl.ds(g * 128, 128), :] = (wide * gain_row).astype(BF16)
-        column = jnp.sum(wide * wide, axis=1, keepdims=True)
-        sums[tp, pl.ds(g, 1), :] = jnp.sum(column * eye, axis=0, keepdims=True)
 
     pl.semaphore_wait(barrier, len(greeted))
 
@@ -219,8 +216,15 @@
             if p in Y_FIRST:
                 cross(p)
 
-    for other in peers:
-        send(sums.at[tp], sums.at[tp], send_s, recv_s.at[tp], other).start()
+    def share_sums():
+        sums[tp] = jnp.zeros((8, 128), F32)
+        for g in range(4):
+            wide = hidden[pl.ds(g * 128, 128), :].astype(F32)
+            column = jnp.sum(wide * wide, axis=1, keepdims=True)
+            sums[tp, pl.ds(g, 1), :] = jnp.sum(column * eye, axis=0, keepdims=True)
+        for other in peers:
+            send(sums.at[tp], sums.at[tp], send_s, recv_s.at[tp], other).start()
+
 
     def wo_block(quarter):
         return wo.at[pl.ds(1, 3), pl.ds(pl.multiple_of(lax.rem(z + quarter, 4) * 128, 128), 128), :]
@@ -347,10 +351,12 @@
     def _():
         weight_steps()
         wo_spread()
+        share_sums()
         fill_tables()
 
     @pl.when(relays_x)
     def _():
+        share_sums()
         fill_tables()
         relay_ring(0, 0)
         relay_ring(0, 1)

time: 147 us -> 147 us (level)
  no operation moved by 1% of the time
where the time goes in v5:
time: 147 us; the launch traced here: 146 us
  Pallas kernels  144 us (98%)
  local copies, waits for them, and re-layouts  2.26 us (2%)
    pallas_call x1, Pallas kernels, local(): pl.pallas_call(body, out_shape=jax.ShapeDtypeStruct((ROWS, FEATS), BF16),...  144 us

profile of v5, /device:TPU:1, one launch (start us, length us, event | category | flops | bytes accessed | tf_op | source)
XLA Modules:
  0.0 146.0 jit_solution(5164236496103873793)
XLA Ops:
  0.0 143.7 %shard_map.55 = bf16[512,1024]{1,0:T(8,128)(2,1)} custom-call(bf16[512,1024]{1,0:T(8,128)(2,1)} %hidden.1, s32[1,4]{1,0:T(1,128)} %lengths.1, f32[8192]{0:T(1024)} %gain.1, bf16[1,8192,768]{2,1,0:T(8,128)(2,1)} %w_in.1, bf16[512,8192]{1,0:T(8,128)(2,1)} %wo_in.1), custom_call_target="tpu_custom_call" | custom-call | tf_op jit(solution)/shard_map/pallas_call | solution.py:576
  143.7 2.3 %copy.7 = bf16[512,1024]{1,0:T(8,128)(2,1)} copy(bf16[512,1024]{1,0:T(8,128)(2,1)} %shard_map.55) | data formatting | bytes 2097152
